TPU v7x, 256 devices: a whole 4x4x8 slice. The times are simulated.
256 devices in a mesh: blk: 16 (over y_hi, z), frames: 16 (over x, y_lo, core).
Axes of the slice: x: 4, y: 4 (y_hi: 2, y_lo: 2; y = y_hi * 2 + y_lo), z: 8, core: 2. Of those that a mesh axis runs over, the one named last changes fastest.
Arguments:
- coarse_query: bfloat16 [512, 16, 256], P('blk'), may hold values from -125 to 125
- coarse_feat: bfloat16 [64, 8160, 256], P('frames', 'blk'), may hold values from -61 to 61
- fine_query: bfloat16 [512, 128], P(('blk', 'frames')), may hold values from -175 to 175
- fine_tiles: bfloat16 [64, 1024, 64, 128], P('frames', 'blk'), may hold values from -61 to 61
- track_pos: int32 [2, 64, 512], P(None, None, ('blk', 'frames')), may hold values from 0 to 959, as said below
- tile_list: int32 [64, 16, 16, 8], P('frames', 'blk'), may hold values from 0 to 63, as said below
- tile_valid: int32 [64, 16, 16, 8], P('frames', 'blk'), may hold values from 0 to 1, as said below
Outputs:
- coarse_pos: float32 [2, 64, 512], P(None, 'frames', 'blk')
- fine_offset: float32 [2, 64, 512], P(None, None, ('blk', 'frames'))
Inputs may be any that keep to these rules, and one draw needn't show every extreme that they name: `tile_list`: in each list the valid slots come first and name distinct tiles of the group's window; padded slots hold 63; in every frame and group some owner's list is full. `tile_valid`: each list has at least 4 valid slots. `track_pos`: rows lie below 544 and columns below 960.
All inputs are finite; a program needn't handle non-finite values.
Results may differ from a plain program's by a relative error of at most 0.0003.
Values may be sent and summed in bfloat16 or wider, within the bound.
A program may use at most 192 MiB of HBM per device.

v0:
```python
import math
import jax
import jax.numpy as jnp
from jax import lax
from jax.sharding import PartitionSpec as P

GH = 68
GW = 120
TILE = 8
SPREAD = 32.0


def coarse(coarse_query, coarse_feat):
    track_group, heads, channels = coarse_query.shape
    frames_here, region, _ = coarse_feat.shape
    blocks = lax.axis_size("blk")
    scale = 1.0 / math.sqrt(channels)
    start = lax.axis_index("blk") * region
    queries = lax.all_gather(coarse_query.reshape(track_group * heads, channels), "blk", axis=0)
    positions = start + jnp.arange(region, dtype=jnp.int32)
    pos_row = (positions // GW).astype(jnp.float32)
    pos_col = (positions % GW).astype(jnp.float32)
    scores = (
        jnp.einsum("brc,fpc->bfpr", queries, coarse_feat, preferred_element_type=jnp.float32)
        * scale
    )
    top = jnp.max(scores, axis=2)
    weights = jnp.exp(scores - top[:, :, None])
    stats = jnp.stack(
        [
            top,
            jnp.sum(weights, axis=2),
            jnp.sum(weights * pos_row[None, None, :, None], axis=2),
            jnp.sum(weights * pos_col[None, None, :, None], axis=2),
        ],
        axis=1,
    )
    stats = lax.all_to_all(stats, "blk", split_axis=0, concat_axis=0, tiled=True)
    top = jnp.max(stats[:, 0], axis=0, keepdims=True)
    factor = jnp.exp(stats[:, 0] - top)
    total = jnp.sum(stats[:, 1] * factor, axis=0)
    rows = jnp.sum(stats[:, 2] * factor, axis=0) / total
    cols = jnp.sum(stats[:, 3] * factor, axis=0) / total
    rows = jnp.mean(rows.reshape(frames_here, track_group, heads), axis=2)
    cols = jnp.mean(cols.reshape(frames_here, track_group, heads), axis=2)
    return jnp.stack([(rows - (GH - 1) / 2.0) / (GH / 4.0), (cols - (GW - 1) / 2.0) / (GW / 4.0)])


def fine(fine_query, fine_tiles, track_pos, tile_list, tile_valid, region):
    frames_here, tiles, cells, channels = fine_tiles.shape
    owners = tile_list.shape[2]
    owned = fine_query.shape[0]
    start = lax.axis_index("blk") * region
    descs = lax.all_gather(fine_query, "frames", axis=0, tiled=True)
    places = lax.all_to_all(track_pos, "frames", split_axis=1, concat_axis=2, tiled=True).astype(
        jnp.float32
    )
    scores = jnp.einsum(
        "nc,fkc->fnk",
        descs,
        fine_tiles.reshape(frames_here, tiles * cells, channels),
        preferred_element_type=jnp.float32,
    ) * (1.0 / math.sqrt(channels))
    ids = tile_list[:, 0]
    live = tile_valid[:, 0]
    listed = jnp.any((ids[:, :, :, None] == jnp.arange(tiles)) & (live[:, :, :, None] > 0), axis=2)
    listed = jnp.repeat(jnp.repeat(listed, owned, axis=1), cells, axis=2)
    index = jnp.arange(tiles * cells, dtype=jnp.int32)
    cell = start + index // cells
    inner = index % cells
    row = (cell // GW * TILE + inner // TILE).astype(jnp.float32)
    col = (cell % GW * TILE + inner % TILE).astype(jnp.float32)
    away_row = row - places[0][:, :, None]
    away_col = col - places[1][:, :, None]
    scores = scores - (away_row**2 + away_col**2) * (0.5 / (SPREAD * SPREAD))
    scores = jnp.where(listed, scores, -1e30)
    weights = jnp.exp(scores - jnp.max(scores, axis=2, keepdims=True))
    total = jnp.sum(weights, axis=2)
    out = jnp.stack(
        [
            jnp.sum(weights * away_row, axis=2) / total / SPREAD,
            jnp.sum(weights * away_col, axis=2) / total / SPREAD,
        ]
    )
    return lax.all_to_all(out, "frames", split_axis=2, concat_axis=1, tiled=True)


def body(coarse_query, coarse_feat, fine_query, fine_tiles, track_pos, tile_list, tile_valid):
    offset = fine(fine_query, fine_tiles, track_pos, tile_list, tile_valid, coarse_feat.shape[1])
    return (coarse(coarse_query, coarse_feat), offset)


def solution(mesh):
    return jax.shard_map(
        body,
        mesh=mesh,
        in_specs=(
            P("blk", None, None),
            P("frames", "blk", None),
            P(("blk", "frames"), None),
            P("frames", "blk", None, None),
            P(None, None, ("blk", "frames")),
            P("frames", "blk", None, None),
            P("frames", "blk", None, None),
        ),
        out_specs=(P(None, "frames", "blk"), P(None, None, ("blk", "frames"))),
        check_vma=False,
    )
```

profile of v0, /device:TPU:2, one launch (start us, length us, event | category | flops | bytes accessed | tf_op | source)
XLA Modules:
  0.0 203.0 jit_solution(1856049340781756826)
XLA Ops:
  7.2 0.0 all-gather.3.cloned.1.call-start
  7.2 0.7 all-gather.3.cloned.1.call-update
  7.9 1.4 copy.87
  9.3 5.9 %all-to-all-start.1 = ((s32[2,64,2]{2,0,1:T(2,128)}), s32[2,64,2]{2,0,1:T(2,128)S(1)}, u32[]{:S(2)}, u32[]{:S(2)}) async-start(s32[2,64,2]{2,0,1:T(2,128)} %copy.87), calls=%async_computation.1 | async-start | bytes 131072 | tf_op jit(solution)/shard_map/all_to_all | solution.py:55
  15.2 0.8 copy.83
  16.0 0.7 compare_bitcast_fusion
  16.7 0.1 copy.84
  16.8 0.2 fusion.16
  17.1 17.5 %all-gather = bf16[16,2,128]{2,1,0:T(2,128)(2,1)S(1)} all-gather(bf16[1,2,128]{2,1,0:T(2,128)(2,1)} %bitcast.111), channel_id=1, replica_groups=mesh['blk'=16,'frames'=16] {'frames'}, dimensions={0}, use_global_device_ids=true | all-gather | bytes 8704 | tf_op jit(solution)/shard_map/all_gather | solution.py:54
  34.6 1.4 broadcast_in_dim.9
  36.0 2.6 %reshape.202 = pred[4,32,4096]{2,1,0:T(32,128)(4,1)S(1)} reshape(pred[4,32,64,64]{3,2,1,0:T(32,128)(4,1)S(1)} %broadcast_in_dim.9) | data formatting | bytes 1048576 | tf_op jit(solution)/shard_map/reshape | solution.py:67
  38.6 0.0 all-to-all-done.1
  38.6 0.1 copy.88
  38.7 0.1 convert_element_type.42
  38.8 0.1 copy.90
  38.9 0.1 copy.92
  39.0 4.6 %fusion.12 = (f32[4,32]{1,0:T(4,128)S(1)}, f32[4,32]{1,0:T(4,128)S(1)}, f32[4,32]{1,0:T(4,128)S(1)}) fusion(f32[4,32]{1,0:T(4,128)S(1)} %copy.90, f32[4096]{0:T(1024)S(1)} %get-tuple-element.19, f32[4,32]{1,0:T(4,128)S(1)} %copy.92, f32[4096]{0:T(1024)S(1)} %get-tuple-element.20, pred[4,32,4096]{2,1,0:T(32,128)(4,1)S(1)} %reshape.202, ...), kind=kOutput, calls=%fused_computation.21 | convolution fusion | flops 143134464 | bytes 4762112 | tf_op jit(solution)/shard_map/sub | solution.py:77
  43.6 0.7 copy.93
  44.3 6.0 %all-to-all-start.2 = ((f32[2,4,32]{1,0,2:T(2,128)}), f32[2,4,32]{1,0,2:T(2,128)S(1)}, u32[]{:S(2)}, u32[]{:S(2)}) async-start(f32[2,4,32]{1,0,2:T(2,128)} %copy.93), calls=%async_computation.2 | async-start | bytes 65536 | tf_op jit(solution)/shard_map/all_to_all | solution.py:85
  50.3 63.3 %all-gather.3.cloned.1.call-done = bf16[16,512,256]{2,1,0:T(8,128)(2,1)} async-done(((bf16[1,512,256]{2,1,0:T(8,128)(2,1)}), bf16[16,512,256]{2,1,0:T(8,128)(2,1)}) %all-gather.3.cloned.1.call-update) | async-done | bytes 4194320 | tf_op jit(solution)/shard_map/all_gather | solution.py:19
  113.6 25.3 %bitcast_reduce_fusion = (f32[16,4,512]{2,0,1:T(8,128)S(1)}, f32[4,510,16,512]{3,1,2,0:T(8,128)}) fusion(bf16[16,512,256]{2,1,0:T(8,128)(2,1)} %all-gather.3.cloned.1.call-done, bf16[4,510,256,1]{2,0,1,3:T(4,128)(2,1)S(1)} %bitcast.99), kind=kOutput, calls=%fused_computation.2 | convolution fusion | flops 8589770752 | bytes 72216576 | tf_op jit(solution)/shard_map/brc,fpc->bfpr/dot_general | solution.py:24
  138.9 36.5 %fusion.2 = (f32[16,4,512]{2,0,1:T(8,128)S(1)}, f32[16,4,512]{2,0,1:T(8,128)S(1)}, f32[16,4,512]{2,0,1:T(8,128)S(1)}) fusion(f32[4,510,16,512]{3,1,2,0:T(8,128)} %get-tuple-element.18, f32[16,4,512]{2,0,1:T(8,128)S(1)} %get-tuple-element.17, f32[510]{0:T(512)S(1)} %get-tuple-element.22, f32[510]{0:T(512)S(1)} %get-tuple-element.21), kind=kLoop, calls=%fused_computation.6 | loop fusion | flops 116883456 | bytes 67375088 | tf_op jit(solution)/shard_map/reduce_sum | solution.py:32
  175.5 1.1 copy.79
  176.7 4.2 %all-to-all-start = ((f32[16,4,4,512]{3,2,1,0:T(4,128)}), f32[16,4,4,512]{3,2,1,0:T(4,128)S(1)}, u32[]{:S(2)}, u32[]{:S(2)}) async-start(f32[16,4,4,512]{3,2,1,0:T(4,128)} %copy.79), calls=%async_computation | async-start | bytes 1048576 | tf_op jit(solution)/shard_map/all_to_all | solution.py:38
  180.9 0.7 all_to_all.28
  181.5 13.4 %all-to-all-done = f32[16,4,4,512]{3,2,1,0:T(4,128)S(1)} async-done(((f32[16,4,4,512]{3,2,1,0:T(4,128)}), f32[16,4,4,512]{3,2,1,0:T(4,128)S(1)}, u32[]{:S(2)}, u32[]{:S(2)}) %all-to-all-start) | async-done | bytes 524320 | tf_op jit(solution)/shard_map/all_to_all | solution.py:38
  195.0 0.1 fusion.22
  195.1 0.1 div.112
  195.2 0.1 reduce_sum.106
  195.3 0.1 div.106
  195.4 0.1 reduce_sum.104
  195.5 0.6 pad_maximum_fusion.1
  (21 shorter events, 0.3 us)
Async XLA Ops:
  7.2 106.4 %all-gather.3.cloned.1.call-start = ((), (), s32[]{:S(2)}) async-start(), calls=%async_computation.3 | async-start | bytes 4456448 | tf_op jit(solution)/shard_map/all_gather | solution.py:19
  9.3 29.3 %all-to-all-start.1 = ((s32[2,64,2]{2,0,1:T(2,128)}), s32[2,64,2]{2,0,1:T(2,128)S(1)}, u32[]{:S(2)}, u32[]{:S(2)}) async-start(s32[2,64,2]{2,0,1:T(2,128)} %copy.87), calls=%async_computation.1 | async-start | bytes 131072 | tf_op jit(solution)/shard_map/all_to_all | solution.py:55
  39.0 74.6 %copy-start = (bf16[4,510,256]{2,0,1:T(4,128)(2,1)S(1)}, bf16[4,510,256]{2,0,1:T(4,128)(2,1)}, u32[]{:S(2)}) copy-start(bf16[4,510,256]{2,0,1:T(4,128)(2,1)} %param.8) | copy-start | bytes 3133444
  44.3 132.3 %all-to-all-start.2 = ((f32[2,4,32]{1,0,2:T(2,128)}), f32[2,4,32]{1,0,2:T(2,128)S(1)}, u32[]{:S(2)}, u32[]{:S(2)}) async-start(f32[2,4,32]{1,0,2:T(2,128)} %copy.93), calls=%async_computation.2 | async-start | bytes 65536 | tf_op jit(solution)/shard_map/all_to_all | solution.py:85
  176.7 18.3 %all-to-all-start = ((f32[16,4,4,512]{3,2,1,0:T(4,128)}), f32[16,4,4,512]{3,2,1,0:T(4,128)S(1)}, u32[]{:S(2)}, u32[]{:S(2)}) async-start(f32[16,4,4,512]{3,2,1,0:T(4,128)} %copy.79), calls=%async_computation | async-start | bytes 1048576 | tf_op jit(solution)/shard_map/all_to_all | solution.py:38
Sparse Core Ops, SparseCore 0:
  10.6 102.9 all-gather.2
where the time goes:
time: 203 us
  waiting for transfers between devices  77.4 us (38%)
  other arithmetic  38.6 us (19%)
  matrix products  29.9 us (15%)
  blocking collectives  17.5 us (9%)
  starting transfers between devices  16.1 us (8%)
  between operations  14.2 us (7%)
  local copies, waits for them, and re-layouts  9.39 us (5%)
    all_gather x1, waiting for transfers between devices, coarse(): lax.all_gather(coarse_query.reshape(track_group * heads, channels), 'blk'...  63.3 us
    reduce_sum x1, other arithmetic, coarse(): jnp.sum(weights, axis=2)  36.5 us
    dot_general x1, matrix products, coarse(): jnp.einsum('brc,fpc->bfpr', queries, coarse_feat, preferred_element_type=...  25.3 us
    all_gather x1, blocking collectives, fine(): descs = lax.all_gather(fine_query, 'frames', axis=0, tiled=True)  17.5 us
    all_to_all x1, waiting for transfers between devices, coarse(): lax.all_to_all(stats, 'blk', split_axis=0, concat_axis=0, tiled=True)  13.4 us
    all_to_all x1, starting transfers between devices, fine(): lax.all_to_all(out, 'frames', split_axis=2, concat_axis=1, tiled=True)  5.99 us
    all_to_all x1, starting transfers between devices, fine(): lax.all_to_all(track_pos, 'frames', split_axis=1, concat_axis=2, tiled=True)  5.86 us
    sub x1, matrix products, fine(): weights = jnp.exp(scores - jnp.max(scores, axis=2, keepdims=True))  4.61 us
  transfers between devices with their start and end apart: 4, of which 2 were waited for; matrix products, arithmetic and copies ran while one was open for 37% of the time, Pallas kernels for 0%

commit v1 on v0

--- a/solution.py
+++ b/solution.py
@@ -51,7 +51,9 @@
     owners = tile_list.shape[2]
     owned = fine_query.shape[0]
     start = lax.axis_index("blk") * region
-    descs = lax.all_gather(fine_query, "frames", axis=0, tiled=True)
+    descs = jnp.concatenate(
+        lax.all_to_all(jnp.stack([fine_query] * lax.axis_size("frames")), "frames", 0, 0), axis=0
+    )
     places = lax.all_to_all(track_pos, "frames", split_axis=1, concat_axis=2, tiled=True).astype(
         jnp.float32
     )

time: 203 us -> 204 us (level)
  blocking collectives: 17.5 us -> 0 us
  waiting for transfers between devices: 77.4 us -> 89.6 us
  starting transfers between devices: 16.1 us -> 20.5 us
    all_gather x1 -> x0, blocking collectives: 17.5 us -> none  [fine(): descs = lax.all_gather(fine_query, 'frames', axis=0, tiled=True)]
    all_gather x1, waiting for transfers between devices: 63.3 us -> 71.2 us  [coarse(): lax.all_gather(coarse_query.reshape(track_group * heads, channels), 'blk'...]
    all_to_all x0 -> x1, starting transfers between devices: none -> 5.72 us  [fine(): lax.all_to_all(jnp.stack([fine_query] * lax.axis_size('frames')), 'frames...]
    all_to_all x0 -> x1, waiting for transfers between devices: none -> 4.29 us  [fine(): lax.all_to_all(jnp.stack([fine_query] * lax.axis_size('frames')), 'frames...]
  transfers between devices with their start and end apart: 4 -> 5, of which waited for: 2 -> 3; matrix products, arithmetic and copies ran while one was open for 37% -> 38% of each run, Pallas kernels for 0% -> 0%
where the time goes in v1:
time: 204 us; the launch traced here: 203 us
  waiting for transfers between devices  89.6 us (44%)
  other arithmetic  38.6 us (19%)
  matrix products  30 us (15%)
  starting transfers between devices  20.5 us (10%)
  between operations  14.2 us (7%)
  local copies, waits for them, and re-layouts  10 us (5%)
    all_gather x1, waiting for transfers between devices, coarse(): lax.all_gather(coarse_query.reshape(track_group * heads, channels), 'blk'...  71.2 us
    reduce_sum x1, other arithmetic, coarse(): jnp.sum(weights, axis=2)  36.5 us
    dot_general x1, matrix products, coarse(): jnp.einsum('brc,fpc->bfpr', queries, coarse_feat, preferred_element_type=...  25.3 us
    all_to_all x1, waiting for transfers between devices, coarse(): lax.all_to_all(stats, 'blk', split_axis=0, concat_axis=0, tiled=True)  13.4 us
    all_to_all x1, starting transfers between devices, fine(): lax.all_to_all(track_pos, 'frames', split_axis=1, concat_axis=2, tiled=True)  5.86 us
    all_to_all x1, starting transfers between devices, fine(): lax.all_to_all(jnp.stack([fine_query] * lax.axis_size('frames')), 'frames...  5.72 us
    all_to_all x1, starting transfers between devices, fine(): lax.all_to_all(out, 'frames', split_axis=2, concat_axis=1, tiled=True)  4.74 us
    sub x1, matrix products, fine(): weights = jnp.exp(scores - jnp.max(scores, axis=2, keepdims=True))  4.66 us
  transfers between devices with their start and end apart: 5, of which 3 were waited for; matrix products, arithmetic and copies ran while one was open for 38% of the time, Pallas kernels for 0%

profile of v1, /device:TPU:2, one launch (start us, length us, event | category | flops | bytes accessed | tf_op | source)
XLA Modules:
  0.0 203.0 jit_solution(5525858089319309331)
XLA Ops:
  7.2 0.7 all-gather.2.cloned.1.call-update
  7.9 1.4 copy.87
  9.3 5.9 %all-to-all-start.2 = ((s32[2,64,2]{2,0,1:T(2,128)}), s32[2,64,2]{2,0,1:T(2,128)S(1)}, u32[]{:S(2)}, u32[]{:S(2)}) async-start(s32[2,64,2]{2,0,1:T(2,128)} %copy.87), calls=%async_computation.2 | async-start | bytes 131072 | tf_op jit(solution)/shard_map/all_to_all | solution.py:57
  15.2 0.8 copy.83
  16.0 0.7 compare_bitcast_fusion
  16.7 0.1 copy.84
  16.8 0.2 fusion.16
  17.1 1.4 broadcast_in_dim.9
  18.5 2.7 %reshape.207 = pred[4,32,4096]{2,1,0:T(32,128)(4,1)S(1)} reshape(pred[4,32,64,64]{3,2,1,0:T(32,128)(4,1)S(1)} %broadcast_in_dim.9) | data formatting | bytes 1048576 | tf_op jit(solution)/shard_map/reshape | solution.py:69
  21.2 0.6 stack.22
  21.8 5.7 %all-to-all-start.1 = ((bf16[16,2,128]{2,1,0:T(2,128)(2,1)}), bf16[16,2,128]{2,1,0:T(2,128)(2,1)S(1)}, u32[]{:S(2)}, u32[]{:S(2)}) async-start(bf16[16,2,128]{2,1,0:T(2,128)(2,1)} %stack.22), calls=%async_computation.1 | async-start | bytes 16384 | tf_op jit(solution)/shard_map/all_to_all | solution.py:55
  27.5 0.1 copy.88
  27.6 0.1 convert_element_type.42
  27.8 0.1 copy.90
  27.9 0.1 copy.92
  27.9 4.3 %all-to-all-done.1 = bf16[16,2,128]{2,1,0:T(2,128)(2,1)S(1)} async-done(((bf16[16,2,128]{2,1,0:T(2,128)(2,1)}), bf16[16,2,128]{2,1,0:T(2,128)(2,1)S(1)}, u32[]{:S(2)}, u32[]{:S(2)}) %all-to-all-start.1) | async-done | bytes 8224 | tf_op jit(solution)/shard_map/all_to_all | solution.py:55
  32.2 4.7 %fusion.12 = (f32[4,32]{1,0:T(4,128)S(1)}, f32[4,32]{1,0:T(4,128)S(1)}, f32[4,32]{1,0:T(4,128)S(1)}) fusion(f32[4,32]{1,0:T(4,128)S(1)} %copy.90, f32[4096]{0:T(1024)S(1)} %get-tuple-element.19, f32[4,32]{1,0:T(4,128)S(1)} %copy.92, f32[4096]{0:T(1024)S(1)} %get-tuple-element.20, pred[4,32,4096]{2,1,0:T(32,128)(4,1)S(1)} %reshape.207, ...), kind=kOutput, calls=%fused_computation.21 | convolution fusion | flops 143134464 | bytes 4762112 | tf_op jit(solution)/shard_map/sub | solution.py:79
  36.9 0.7 copy.93
  37.6 4.7 %all-to-all-start.3 = ((f32[2,4,32]{1,0,2:T(2,128)}), f32[2,4,32]{1,0,2:T(2,128)S(1)}, u32[]{:S(2)}, u32[]{:S(2)}) async-start(f32[2,4,32]{1,0,2:T(2,128)} %copy.93), calls=%async_computation.3 | async-start | bytes 65536 | tf_op jit(solution)/shard_map/all_to_all | solution.py:87
  42.4 71.2 %all-gather.2.cloned.1.call-done = bf16[16,512,256]{2,1,0:T(8,128)(2,1)} async-done(((bf16[1,512,256]{2,1,0:T(8,128)(2,1)}), bf16[16,512,256]{2,1,0:T(8,128)(2,1)}) %all-gather.2.cloned.1.call-update) | async-done | bytes 4194320 | tf_op jit(solution)/shard_map/all_gather | solution.py:19
  113.6 25.3 %bitcast_reduce_fusion = (f32[16,4,512]{2,0,1:T(8,128)S(1)}, f32[4,510,16,512]{3,1,2,0:T(8,128)}) fusion(bf16[16,512,256]{2,1,0:T(8,128)(2,1)} %all-gather.2.cloned.1.call-done, bf16[4,510,256,1]{2,0,1,3:T(4,128)(2,1)S(1)} %bitcast.98), kind=kOutput, calls=%fused_computation.2 | convolution fusion | flops 8589770752 | bytes 72216576 | tf_op jit(solution)/shard_map/brc,fpc->bfpr/dot_general | solution.py:24
  138.9 36.5 %fusion.2 = (f32[16,4,512]{2,0,1:T(8,128)S(1)}, f32[16,4,512]{2,0,1:T(8,128)S(1)}, f32[16,4,512]{2,0,1:T(8,128)S(1)}) fusion(f32[4,510,16,512]{3,1,2,0:T(8,128)} %get-tuple-element.18, f32[16,4,512]{2,0,1:T(8,128)S(1)} %get-tuple-element.17, f32[510]{0:T(512)S(1)} %get-tuple-element.22, f32[510]{0:T(512)S(1)} %get-tuple-element.21), kind=kLoop, calls=%fused_computation.6 | loop fusion | flops 116883456 | bytes 67375088 | tf_op jit(solution)/shard_map/reduce_sum | solution.py:32
  175.5 1.1 copy.79
  176.7 4.2 %all-to-all-start = ((f32[16,4,4,512]{3,2,1,0:T(4,128)}), f32[16,4,4,512]{3,2,1,0:T(4,128)S(1)}, u32[]{:S(2)}, u32[]{:S(2)}) async-start(f32[16,4,4,512]{3,2,1,0:T(4,128)} %copy.79), calls=%async_computation | async-start | bytes 1048576 | tf_op jit(solution)/shard_map/all_to_all | solution.py:38
  180.9 0.7 all_to_all.32
  181.5 13.4 %all-to-all-done = f32[16,4,4,512]{3,2,1,0:T(4,128)S(1)} async-done(((f32[16,4,4,512]{3,2,1,0:T(4,128)}), f32[16,4,4,512]{3,2,1,0:T(4,128)S(1)}, u32[]{:S(2)}, u32[]{:S(2)}) %all-to-all-start) | async-done | bytes 524320 | tf_op jit(solution)/shard_map/all_to_all | solution.py:38
  195.0 0.1 fusion.22
  195.1 0.1 div.112
  195.2 0.1 reduce_sum.106
  195.3 0.1 div.106
  195.4 0.1 reduce_sum.104
  195.5 0.6 pad_maximum_fusion.1
  (25 shorter events, 0.3 us)
Async XLA Ops:
  7.2 14.1 %copy-start.1 = (bf16[2,128]{1,0:T(2,128)(2,1)S(1)}, bf16[2,128]{1,0:T(2,128)(2,1)}, u32[]{:S(2)}) copy-start(bf16[2,128]{1,0:T(2,128)(2,1)} %param.9) | copy-start | bytes 1540
  7.2 106.4 %all-gather.2.cloned.1.call-start = ((), (), s32[]{:S(2)}) async-start(), calls=%async_computation.4 | async-start | bytes 4456448 | tf_op jit(solution)/shard_map/all_gather | solution.py:19
  9.3 11.9 %all-to-all-start.2 = ((s32[2,64,2]{2,0,1:T(2,128)}), s32[2,64,2]{2,0,1:T(2,128)S(1)}, u32[]{:S(2)}, u32[]{:S(2)}) async-start(s32[2,64,2]{2,0,1:T(2,128)} %copy.87), calls=%async_computation.2 | async-start | bytes 131072 | tf_op jit(solution)/shard_map/all_to_all | solution.py:57
  21.8 10.4 %all-to-all-start.1 = ((bf16[16,2,128]{2,1,0:T(2,128)(2,1)}), bf16[16,2,128]{2,1,0:T(2,128)(2,1)S(1)}, u32[]{:S(2)}, u32[]{:S(2)}) async-start(bf16[16,2,128]{2,1,0:T(2,128)(2,1)} %stack.22), calls=%async_computation.1 | async-start | bytes 16384 | tf_op jit(solution)/shard_map/all_to_all | solution.py:55
  32.2 81.4 %copy-start = (bf16[4,510,256]{2,0,1:T(4,128)(2,1)S(1)}, bf16[4,510,256]{2,0,1:T(4,128)(2,1)}, u32[]{:S(2)}) copy-start(bf16[4,510,256]{2,0,1:T(4,128)(2,1)} %param.8) | copy-start | bytes 3133444
  37.6 139.0 %all-to-all-start.3 = ((f32[2,4,32]{1,0,2:T(2,128)}), f32[2,4,32]{1,0,2:T(2,128)S(1)}, u32[]{:S(2)}, u32[]{:S(2)}) async-start(f32[2,4,32]{1,0,2:T(2,128)} %copy.93), calls=%async_computation.3 | async-start | bytes 65536 | tf_op jit(solution)/shard_map/all_to_all | solution.py:87
  176.7 18.3 %all-to-all-start = ((f32[16,4,4,512]{3,2,1,0:T(4,128)}), f32[16,4,4,512]{3,2,1,0:T(4,128)S(1)}, u32[]{:S(2)}, u32[]{:S(2)}) async-start(f32[16,4,4,512]{3,2,1,0:T(4,128)} %copy.79), calls=%async_computation | async-start | bytes 1048576 | tf_op jit(solution)/shard_map/all_to_all | solution.py:38
Sparse Core Ops, SparseCore 0:
  10.6 102.9 all-gather.1
